TPU v7x, 32 devices: a whole 2x2x4 slice. The times are simulated.
32 devices in a mesh: rows: 16 (over z, y, core), blk: 2 (over x).
Axes of the slice: x: 2, y: 2, z: 4, core: 2. Of those that a mesh axis runs over, the one named last changes fastest.
Arguments:
- hidden: bfloat16 [16, 768, 1280], P('rows', 'blk'), may hold values from -6 to 6
- starts: int32 [16, 4], P('rows'), may hold values from 0 to 767, as said below
- first_gain: float32 [1280], replicated, may hold values from 0.5 to 2
- first_shift: float32 [1280], replicated, may hold values from -3 to 3
- qkv_weight: bfloat16 [1280, 3840], P('rows'), may hold values from -0.15625 to 0.15625
- out_weight: bfloat16 [1280, 1280], P('rows'), may hold values from -0.625 to 0.625
- second_gain: float32 [1280], replicated, may hold values from 0.5 to 2
- second_shift: float32 [1280], replicated, may hold values from -3 to 3
- up_weight: bfloat16 [1280, 5120], P('rows'), may hold values from -0.15625 to 0.15625
- hidden_bias: float32 [5120], replicated, may hold values from -3 to 3
- down_weight: bfloat16 [5120, 1280], P('rows'), may hold values from -0.078125 to 0.078125
- cotangent: bfloat16 [16, 768, 1280], P('rows', 'blk'), may hold values from -6 to 6
Outputs:
- output: float32 [16, 768, 1280], P('rows', 'blk')
- grad_hidden: float32 [16, 768, 1280], P('rows', 'blk')
- grad_qkv: float32 [1280, 3840], P('rows')
- grad_out: float32 [1280, 1280], P('rows')
- grad_up: float32 [1280, 5120], P('rows')
- grad_down: float32 [5120, 1280], P('rows')
- grad_first_gain: float32 [1280], replicated
- grad_first_shift: float32 [1280], replicated
- grad_second_gain: float32 [1280], replicated
- grad_second_shift: float32 [1280], replicated
- grad_hidden_bias: float32 [5120], replicated
Inputs may be any that keep to these rules, and one draw needn't show every extreme that they name: Each row of starts lists the first positions (CLS tokens) of its 4 cells in increasing order, beginning with 0; every cell holds one position or more, and a cell runs up to the next start (the last up to 768). In every row one cell begins among the first 384 positions and ends among the last 384.
All inputs are finite; a program needn't handle non-finite values.
Results may differ from a plain program's by a relative error of at most 0.02.
Values may be sent and summed in bfloat16 or wider, within the bound.
A program may use at most 256 MiB of HBM per device.

v0:
```python
import functools
import math

import jax
import jax.numpy as jnp
from jax import lax
from jax.experimental import pallas as pl
from jax.experimental.pallas import tpu as pltpu
from jax.sharding import PartitionSpec as P

HEADS = 20
HEAD_DIM = 64


masked_score = -1e30
block_limit = 512


def layer_norm(values, gain, shift):
    mean_value = jnp.mean(values, axis=-1, keepdims=True)
    centred = values - mean_value
    variance = jnp.mean(centred * centred, axis=-1, keepdims=True)
    return centred * lax.rsqrt(variance + 1e-05) * gain + shift


def segment_of(starts_row, positions):
    reached = starts_row[None, :] <= positions[:, None]
    return jnp.sum(reached.astype(jnp.int32), axis=1) - 1


def scores_with_mask(queries, key_block, query_seg, key_seg):
    products = jnp.einsum("qhe,khe->hqk", queries, key_block, preferred_element_type=jnp.float32)
    products = products * queries.shape[2] ** (-0.5)
    allowed = (query_seg[:, None] == key_seg[None, :])[None, :, :]
    return (jnp.where(allowed, products, masked_score), allowed)


def attend_rows(running, key_rows, value_rows, queries, query_seg, starts_row):
    piece_rows = key_rows.shape[0]
    step_rows = math.gcd(piece_rows, block_limit)
    head_count = queries.shape[1]
    head_width = queries.shape[2]

    def one_block(block_index, state):
        row_top, denominator, weighted = state
        block_start = block_index * step_rows
        key_block = lax.dynamic_slice_in_dim(key_rows, block_start, step_rows, 0).reshape(
            step_rows, head_count, head_width
        )
        value_block = lax.dynamic_slice_in_dim(value_rows, block_start, step_rows, 0).reshape(
            step_rows, head_count, head_width
        )
        key_seg = segment_of(starts_row, block_start + jnp.arange(step_rows, dtype=jnp.int32))
        scores, allowed = scores_with_mask(queries, key_block, query_seg, key_seg)
        new_top = jnp.maximum(row_top, jnp.max(scores, axis=-1))
        factor = jnp.exp(row_top - new_top)
        weights = jnp.where(allowed, jnp.exp(scores - new_top[:, :, None]), 0.0)
        denominator = denominator * factor + jnp.sum(weights, axis=-1)
        weighted = weighted * factor[:, :, None] + jnp.einsum(
            "hqk,khe->hqe",
            weights.astype(jnp.bfloat16),
            value_block,
            preferred_element_type=jnp.float32,
        )
        return (new_top, denominator, weighted)

    return lax.fori_loop(0, piece_rows // step_rows, one_block, running)


def on_device(
    hidden,
    starts,
    first_gain,
    first_shift,
    qkv_weight,
    out_weight,
    second_gain,
    second_shift,
    up_weight,
    hidden_bias,
    down_weight,
    cotangent,
):
    rows_here = hidden.shape[1]
    model_width = hidden.shape[2]
    head_count = HEADS
    head_width = HEAD_DIM
    score_scale = head_width ** (-0.5)
    inputs = hidden[0].astype(jnp.float32)
    starts_row = starts[0]
    offset = lax.axis_index("blk") * rows_here
    query_seg = segment_of(starts_row, offset + jnp.arange(rows_here, dtype=jnp.int32))
    qkv_full, out_full, up_full, down_full = (
        lax.all_gather(qkv_weight, "rows", axis=0, tiled=True),
        lax.all_gather(out_weight, "rows", axis=0, tiled=True),
        lax.all_gather(up_weight, "rows", axis=0, tiled=True),
        lax.all_gather(down_weight, "rows", axis=0, tiled=True),
    )
    normed_low = layer_norm(inputs, first_gain, first_shift).astype(jnp.bfloat16)
    packed = jnp.dot(normed_low, qkv_full, preferred_element_type=jnp.float32).astype(jnp.bfloat16)
    queries = packed[:, :model_width].reshape(rows_here, head_count, head_width)
    key_rows = packed[:, model_width : 2 * model_width]
    value_rows = packed[:, 2 * model_width :]
    initial = (
        jnp.full((head_count, rows_here), masked_score, jnp.float32),
        jnp.zeros((head_count, rows_here), jnp.float32),
        jnp.zeros((head_count, rows_here, head_width), jnp.float32),
    )
    row_top, denominator, weighted = attend_rows(
        initial,
        lax.all_gather(key_rows, "blk", axis=0, tiled=True),
        lax.all_gather(value_rows, "blk", axis=0, tiled=True),
        queries,
        query_seg,
        starts_row,
    )
    log_total = row_top + jnp.log(denominator)
    attended = jnp.transpose(weighted / denominator[:, :, None], (1, 0, 2))
    attended_low = attended.reshape(rows_here, model_width).astype(jnp.bfloat16)
    residual = inputs + jnp.dot(attended_low, out_full, preferred_element_type=jnp.float32)
    second_low = layer_norm(residual, second_gain, second_shift).astype(jnp.bfloat16)
    up_values = jnp.dot(second_low, up_full, preferred_element_type=jnp.float32) + hidden_bias
    activated_low = jax.nn.gelu(up_values, approximate=False).astype(jnp.bfloat16)
    output = residual + jnp.dot(activated_low, down_full, preferred_element_type=jnp.float32)
    cot_low = cotangent[0]
    d_activated = jnp.einsum("tc,fc->tf", cot_low, down_full, preferred_element_type=jnp.float32)
    unused_gelu, gelu_pull = jax.vjp(
        lambda values: jax.nn.gelu(values, approximate=False), up_values
    )
    d_up_low = gelu_pull(d_activated)[0].astype(jnp.bfloat16)
    d_second = jnp.einsum("tf,cf->tc", d_up_low, up_full, preferred_element_type=jnp.float32)
    unused_second, second_pull = jax.vjp(layer_norm, residual, second_gain, second_shift)
    d_norm_two, d_second_gain, d_second_shift = second_pull(d_second)
    d_residual = cot_low.astype(jnp.float32) + d_norm_two
    d_branch_low = d_residual.astype(jnp.bfloat16)
    d_attended_low = jnp.einsum(
        "tc,kc->tk", d_branch_low, out_full, preferred_element_type=jnp.float32
    ).astype(jnp.bfloat16)
    d_attended3 = d_attended_low.reshape(rows_here, head_count, head_width)
    row_dots = jnp.einsum("qhe,qhe->hq", d_attended3.astype(jnp.float32), attended)
    keys_all, values_all = (
        lax.all_gather(key_rows, "blk", axis=0, tiled=True),
        lax.all_gather(value_rows, "blk", axis=0, tiled=True),
    )
    length = keys_all.shape[0]
    step_rows = math.gcd(length, block_limit)

    def block_terms(block_index):
        block_start = block_index * step_rows
        key_block = lax.dynamic_slice_in_dim(keys_all, block_start, step_rows, 0).reshape(
            step_rows, head_count, head_width
        )
        value_block = lax.dynamic_slice_in_dim(values_all, block_start, step_rows, 0).reshape(
            step_rows, head_count, head_width
        )
        key_seg = segment_of(starts_row, block_start + jnp.arange(step_rows, dtype=jnp.int32))
        scores, allowed = scores_with_mask(queries, key_block, query_seg, key_seg)
        probability = jnp.where(allowed, jnp.exp(scores - log_total[:, :, None]), 0.0)
        d_probs = jnp.einsum(
            "qhe,khe->hqk", d_attended3, value_block, preferred_element_type=jnp.float32
        )
        d_scores = (probability * (d_probs - row_dots[:, :, None])).astype(jnp.bfloat16)
        return (key_block, probability, d_scores)

    dq_start = jnp.zeros((rows_here, head_count, head_width), jnp.float32)

    def back_block(dq_sum, block_index):
        key_block, probability, d_scores = block_terms(block_index)
        dq_sum = dq_sum + jnp.einsum(
            "hqk,khe->qhe", d_scores, key_block, preferred_element_type=jnp.float32
        )
        dk_block = (
            jnp.einsum("hqk,qhe->khe", d_scores, queries, preferred_element_type=jnp.float32)
            * score_scale
        )
        dv_block = jnp.einsum(
            "hqk,qhe->khe",
            probability.astype(jnp.bfloat16),
            d_attended3,
            preferred_element_type=jnp.float32,
        )
        return (
            dq_sum,
            (dk_block.reshape(step_rows, model_width), dv_block.reshape(step_rows, model_width)),
        )

    dq_sum, (dk_terms, dv_terms) = lax.scan(back_block, dq_start, jnp.arange(length // step_rows))
    dk_rows, dv_rows = (
        lax.psum_scatter(
            dk_terms.reshape(length, model_width).astype(jnp.bfloat16),
            "blk",
            scatter_dimension=0,
            tiled=True,
        ).astype(jnp.float32),
        lax.psum_scatter(
            dv_terms.reshape(length, model_width).astype(jnp.bfloat16),
            "blk",
            scatter_dimension=0,
            tiled=True,
        ).astype(jnp.float32),
    )
    d_packed = jnp.concatenate(
        [(dq_sum * score_scale).reshape(rows_here, model_width), dk_rows, dv_rows], axis=1
    ).astype(jnp.bfloat16)
    d_normed = jnp.einsum("tn,cn->tc", d_packed, qkv_full, preferred_element_type=jnp.float32)
    unused_first, first_pull = jax.vjp(layer_norm, inputs, first_gain, first_shift)
    d_norm_one, d_first_gain, d_first_shift = first_pull(d_normed)
    grad_hidden = d_residual + d_norm_one
    d_bias = jnp.sum(d_up_low, axis=0, dtype=jnp.float32)
    wide_share = lax.psum_scatter(
        jnp.concatenate(
            [
                jnp.einsum("tc,tn->cn", normed_low, d_packed, preferred_element_type=jnp.float32),
                jnp.einsum(
                    "tc,tn->cn", attended_low, d_branch_low, preferred_element_type=jnp.float32
                ),
                jnp.einsum("tc,tn->cn", second_low, d_up_low, preferred_element_type=jnp.float32),
            ],
            axis=1,
        ).astype(jnp.bfloat16),
        "rows",
        scatter_dimension=0,
        tiled=True,
    )
    down_share = lax.psum_scatter(
        jnp.einsum("tf,tn->fn", activated_low, cot_low, preferred_element_type=jnp.float32).astype(
            jnp.bfloat16
        ),
        "rows",
        scatter_dimension=0,
        tiled=True,
    )
    wide_grads, down_grads = (
        lax.psum(wide_share, "blk").astype(jnp.float32),
        lax.psum(down_share, "blk").astype(jnp.float32),
    )
    grad_qkv = wide_grads[:, : 3 * model_width]
    grad_out = wide_grads[:, 3 * model_width : 4 * model_width]
    grad_up = wide_grads[:, 4 * model_width :]
    small_grads = lax.psum(
        (d_first_gain, d_first_shift, d_second_gain, d_second_shift, d_bias), ("rows", "blk")
    )
    return (
        output[None],
        grad_hidden[None],
        grad_qkv,
        grad_out,
        grad_up,
        down_grads,
        small_grads[0],
        small_grads[1],
        small_grads[2],
        small_grads[3],
        small_grads[4],
    )


MESH = pl.DeviceIdType.MESH
FORWARD_MOVES = (
    ((0, 0), (1, 0), (2, 0), (0, 1), (1, 1), (2, 1),),
    (),
    (),
    (),
    (),
    (),
    ((2, 3),),
    (),
    (),
    (),
    ((3, 0, 1, 0), (4, 0, 0), (4, 1, 0), (3, 0, 0, 0), (3, 1, 1, 0), (4, 0, 2), (3, 1, 0, 0), (0, 2), (2, 2), (4, 0, 1), (3, 0, 2, 0), (4, 1, 2), (3, 1, 2, 0), (1, 2), (4, 1, 1), (2, 5),),
    (),
    (),
    ((4, 0, 3), (3, 2, 1, 0), (2, 4), (4, 1, 3), (3, 2, 0, 0),),
    (),
    (),
    ((4, 2, 0), (0, 3),),
    ((3, 2, 2, 0), (4, 2, 2), (1, 3),),
    (),
    (),
    (),
    (),
    (),
    (),
    ((4, 2, 1),),
    (),
    (),
    (),
    (),
    (),
    ((3, 3, 1, 0), (4, 2, 3),),
    (),
    (),
    ((3, 3, 0, 0), (4, 3, 0),),
    (),
    (),
    (),
    (),
    (),
    (),
    ((4, 3, 2), (3, 3, 2, 0), (0, 4), (1, 5), (3, 4, 1, 0), (4, 3, 1), (1, 4), (3, 4, 0, 0), (4, 3, 3), (0, 5), (3, 4, 2, 0),),
    (),
    (),
    ((4, 5, 0),),
    ((3, 5, 1, 0),),
    (),
    (),
    ((4, 4, 2),),
    (),
    (),
    ((3, 5, 0, 0),),
    (),
    ((4, 4, 0),),
    (),
    ((3, 5, 1, 1),),
    (),
    ((4, 4, 1),),
    (),
    ((3, 5, 0, 1),),
    ((4, 4, 3),),
    (),
    (),
    ((3, 5, 2, 0),),
    (),
    (),
    (),
    (),
    ((3, 5, 2, 1),),
    (),
    (),
    (),
    (),
    (),
)
ROWS_Z, ROWS_Y = 4, 2
PAIR = 128
UNIT = 640
SLOTS = 2
SPARE = 3


def place_of():
    index = lax.axis_index("rows")
    return index // 4, lax.rem(index // 2, 2), lax.rem(index, 2)


def row_of(z, y, core):
    return (lax.rem(z + ROWS_Z, ROWS_Z) * ROWS_Y + y) * 2 + core


def aligned(index, step):
    return pl.ds(pl.multiple_of(index * step, step), step)


def dot_nt(left, right):
    return lax.dot_general(left, right, (((1,), (1,)), ((), ())), preferred_element_type=jnp.float32)


def dot_nn(left, right):
    return jnp.dot(left, right, preferred_element_type=jnp.float32)


def head_lanes(width):
    lane = lax.broadcasted_iota(jnp.int32, (1, width), 1)
    return (lane < HEAD_DIM, lane >= HEAD_DIM)


def greet(peers):
    barrier = pltpu.get_barrier_semaphore()
    for peer in peers:
        pl.semaphore_signal(barrier, inc=1, device_id=peer, device_id_type=MESH)
    pl.semaphore_wait(barrier, len(peers))


def neighbours():
    z, y, core = place_of()
    return [
        {"rows": row_of(z + 1, y, core)},
        {"rows": row_of(z + 2, y, core)},
        {"rows": row_of(z + 3, y, core)},
        {"rows": row_of(z, 1 - y, core)},
        {"rows": row_of(z, y, 1 - core)},
        {"blk": 1 - lax.axis_index("blk")},
    ]


def write_marks(starts_ref, key_marks, query_marks):
    shape = key_marks.shape
    at = lax.broadcasted_iota(jnp.int32, shape, 0)
    lane = lax.broadcasted_iota(jnp.int32, shape, 1)
    lane = jnp.where(lane < HEAD_DIM, lane, lane - HEAD_DIM) - SPARE
    cell = jnp.zeros(shape, jnp.int32) - 1
    for i in range(starts_ref.shape[1]):
        cell += (at >= starts_ref[0, i]).astype(jnp.int32)
    key_marks[...] = jnp.where((lane == cell) | (lane < 0), 1.0, 0.0).astype(key_marks.dtype)
    blocked = (lane != cell) & (lane >= 0) & (lane < starts_ref.shape[1])
    query_marks[...] = jnp.where(blocked, masked_score, 0.0).astype(query_marks.dtype)


def z_place(z):
    return 2 * lax.rem(z, 2) + z // 2


def grad_chunk(target, left, right):
    def half(j, carry):
        value = dot_nn(left(j), right()).astype(jnp.bfloat16)
        n = value.shape[1]
        rows = value.shape[0] // 8
        for block in range(8):
            to_z, to_y, to_core = block // 4, block // 2 % 2, block % 2
            target[to_core, to_y, 2 * to_z + j, :, :n] = value[block * rows : (block + 1) * rows]
        return carry

    lax.fori_loop(0, 2, half, 0)


def forward_kernel(
    hidden, cot, starts, gain1, shift1, gain2, shift2, bias_in, q_in, o_in, u_in, d_in,
    q_all, o_all, u_all, d_all, dy_all, down_sums, normed_t_out, packed_out, lse_out, att_out, att_t_out, resid_out,
    second_t_out, act_out, slope_out,
    hid_other, normed, wq, wo, wu, packed, key_marks, query_marks, att_part, att_own, resid, second,
    act, act_t, slope, normed_t, att_t, second_t, lse, u_wide, q_own, o_own, u_own, d_own, dy, bias, parts, core_in,
    local_sem, send_sem, recv_sem, x_send, x_recv,
):
    bf16 = jnp.bfloat16
    z, y, core = place_of()
    me = row_of(z, y, core)
    piece = lax.axis_index("blk")
    other = 1 - piece
    own_rows, width = hidden.shape
    length = packed.shape[0]
    rows = o_own.shape[0]
    early = rows * 3 // 5
    d_half = lambda half: pl.ds(half * rows, rows)
    own = (
        q_own.at[pl.ds(0, early)], q_own.at[pl.ds(early, rows - early)], o_own, u_own,
        d_own.at[d_half(0)], d_own.at[d_half(1)],
    )
    last = len(own) - 1

    def slot_of(w, at_z, at_y, at_core):
        slot = row_of(at_z, at_y, at_core)
        if w < 2:
            return q_all.at[slot, pl.ds(w * early, own[w].shape[0])]
        if w < 4:
            return (o_all, u_all)[w - 2].at[slot]
        return d_all.at[slot, d_half(w - 4)]

    x_peer = {"blk": other}
    peers = neighbours()
    pairs = packed.shape[1] // (3 * PAIR)
    first_gain, first_shift, second_gain, second_shift = (
        ref[...].reshape(1, width) for ref in (gain1, shift1, gain2, shift2)
    )

    def local(src, dst, index):
        return pltpu.make_async_copy(src, dst, local_sem.at[index])

    near = z + 1 - 2 * lax.rem(z, 2)
    far = lax.rem(z + 2, ROWS_Z)
    spread = (z, far, near, ROWS_Z - 1 - z)

    def send(w, at_z, v, place, peer, first=False):
        block = slot_of(w, at_z, y if v == 0 else 1 - y, core)
        index = w * 18 + place
        return pltpu.make_async_remote_copy(
            src_ref=own[w] if first else block, dst_ref=block, send_sem=send_sem.at[index],
            recv_sem=recv_sem.at[index], device_id=peer, device_id_type=MESH,
        )

    def along(w, k, v):
        peer = {"rows": row_of(far if k == 0 else near, y, core)}
        return send(w, far if k == 2 else z, v, 2 * k + v, peer, k < 2 and v == 0)

    def to_y(w, at_z, first=False):
        return send(w, at_z, 0, 6 + at_z, peers[3], first)

    def to_core(w, at_z, v, first=False):
        return send(w, at_z, v, 10 + 2 * at_z + v, peers[4], first)

    def pass_on(w, v):
        inner = (z == 1) | (z == 2)

        @pl.when(inner)
        def _():
            along(w, 0, v).start()

        along(w, 1, v).start()

        @pl.when(jnp.logical_not(inner))
        def _():
            along(w, 0, v).start()

    def relay_z(w, k, v):
        along(w, k, v).wait_recv()
        if k == 0:
            along(w, 2, v).start()
        at_z = spread[k + 1]
        if w < last:
            to_y(w, at_z).start()
        to_core(w, at_z, v).start()

    def relay_y(w, k):
        to_y(w, spread[k]).wait_recv()
        to_core(w, spread[k], 1).start()
        if w == last:
            pass_on(w, 1)

    def all_here(ws):
        for w in ws:
            for at_z in range(ROWS_Z):
                for v in range(2):
                    to_core(w, at_z, v).wait_recv()

    def all_here_load(ws, source, target, first):
        for i, at_z in enumerate(spread):
            for v in range(2):
                for w in ws:
                    to_core(w, at_z, v).wait_recv()
                chip = pl.ds(row_of(at_z, y if v == 0 else 1 - y, 0), 2)
                local(source.at[chip], target.at[chip], first + 2 * i + v).start()

    def loaded(source, target, first):
        for i in range(2 * ROWS_Z):
            chip = pl.ds(0, 2)
            local(source.at[chip], target.at[chip], first + i).wait()

    def all_gone(w):
        for v in range(1 if w < last else 2):
            for k in range(3):
                along(w, k, v).wait_send()
        for at_z in range(ROWS_Z) if w < last else (z,):
            to_y(w, at_z).wait_send()
        for at_z in range(ROWS_Z):
            for v in range(2):
                to_core(w, at_z, v).wait_send()

    def to_x(src, dst, index):
        return pltpu.make_async_remote_copy(
            src_ref=src, dst_ref=dst, send_sem=x_send.at[index], recv_sem=x_recv.at[index],
            device_id=x_peer, device_id_type=MESH,
        )

    third = q_in.shape[1] // 3
    share = third // 2
    q_picks = []
    for part in range(3):
        picked = q_in.at[:, pl.ds(pl.multiple_of(part * third + piece * share, 128), share)]
        q_picks.append(local(picked, q_own.at[:, pl.ds(part * share, share)], 17 + part))
        q_picks[-1].start()
    d_mine = d_in.at[pl.ds(piece * 2 * rows, 2 * rows)]
    local(o_in, o_own, 1).start()
    local(u_in, u_wide, 2).start()
    local(d_mine, d_own, 3).start()
    local(cot, dy.at[piece], 4).start()
    greet(peers)
    for copy in q_picks:
        copy.wait()
    hidden_x = to_x(hidden, hid_other, 0)
    cot_x = to_x(cot, dy.at[piece], 1)
    local(o_in, o_own, 1).wait()
    local(d_mine, d_own, 3).wait()
    local(u_in, u_wide, 2).wait()
    half_rows = lambda half: pl.ds(pl.multiple_of(half * own_rows, 128), own_rows)

    def first_copies():
        local(q_own, q_all.at[me], 0).start()
        local(o_own, o_all.at[me], 1).start()
        local(d_own, d_all.at[me], 3).start()
        local(cot, dy.at[piece], 4).wait()

    units_each = 2 * rows
    group = 8 * units_each

    def mine(block):
        wide = block.astype(jnp.float32)
        halves = []
        for half in range(2):
            at = [slice((2 * j + half) * units_each, (2 * j + half + 1) * units_each) for j in range(4)]
            halves.append(jnp.concatenate([wide[:, cols] for cols in at], axis=1))
        return jnp.where(piece == 0, halves[0], halves[1])

    def pick_units(g):
        cols = slice(g * group // 2, (g + 1) * group // 2)
        u_own[:, cols] = mine(u_wide[:, g * group : (g + 1) * group]).astype(bf16)
        bias[:, cols] = mine(bias_in[g * group : (g + 1) * group].reshape(1, group))
        if g == u_own.shape[1] * 2 // group - 1:
            local(u_own, u_all.at[me], 2).start()

    def norm_rows(source, half, part):
        step = 64
        steps = own_rows // step

        def body(i, carry):
            value = source[aligned(i, step), :].astype(jnp.float32)
            low = layer_norm(value, first_gain, first_shift).astype(bf16)
            normed[pl.ds(pl.multiple_of(half * own_rows + i * step, step), step), :] = low
            return carry

        lax.fori_loop(steps * part // 2, steps * (part + 1) // 2, body, 0)

    def q_here():
        local(q_own, q_all.at[me], 0).wait()
        all_here_load((0, 1), q_all, wq, 20)

    def project(begin, end):
        def body(part, carry):
            cols = aligned(part, share)
            value = dot_nn(normed[...], wq[:, :, cols].reshape(width, share)).astype(bf16)
            packed[:, cols] = value * jnp.where(part == 0, HEAD_DIM ** (-0.5), 1.0).astype(bf16)
            return carry

        lax.fori_loop(begin, end, body, 0)
        if end == 3:
            local(packed, packed_out, 9).start()

    first_lanes = head_lanes(PAIR)

    def att_cols(half, p):
        return pl.ds(pl.multiple_of(half * pairs * PAIR + p * PAIR, PAIR), PAIR)

    def attend(p, half):
        at_q, at_k, at_v = (slice(t * share + PAIR * p, t * share + PAIR * (p + 1)) for t in range(3))
        value_t = packed[:, at_v].T
        at = half_rows(half)
        queries = packed[at, at_q]
        keys = packed[:, at_k]
        halves = []
        for h in range(2):
            one = jnp.where(first_lanes[h], queries, query_marks[at, :])
            scores = dot_nt(jnp.where(first_lanes[h], keys, key_marks[...]), one)
            top = jnp.max(scores, axis=0, keepdims=True)
            weights = jnp.exp(scores - top)
            total = jnp.sum(weights, axis=0, keepdims=True)
            lse[2 * p + h : 2 * p + h + 1, at] = top + jnp.log(total)
            summed = dot_nn(value_t[h * HEAD_DIM : (h + 1) * HEAD_DIM], weights.astype(bf16))
            halves.append(summed / total)
        return jnp.concatenate(halves, axis=0).T.astype(bf16)

    def attend_other(p):
        att_part[:, p * PAIR : (p + 1) * PAIR] = attend(p, other)

    def attend_own(p):
        att_own[:, att_cols(piece, p)] = attend(p, piece)
        if p == pairs - 1:
            for copy in att_outs:
                copy.start()

    att_x = [
        to_x(att_part.at[:, pl.ds(p * PAIR, PAIR)], att_own.at[:, att_cols(piece, p)], 2 + p) for p in range(pairs)
    ]

    att_outs = (
        local(att_part, att_out.at[half_rows(other)], 45),
        local(att_own.at[:, pl.ds(pl.multiple_of(piece * share, 128), share)], att_out.at[half_rows(piece)], 46),
    )

    def o_here():
        local(o_own, o_all.at[me], 1).wait()
        all_here_load((2,), o_all, wo, 28)

    def att_here():
        for copy in att_x:
            copy.wait_recv()
        loaded(o_all, wo, 28)

    part_rows = own_rows // 2
    second_x = [
        to_x(second.at[piece, pl.ds(i * part_rows, part_rows)], second.at[piece, pl.ds(i * part_rows, part_rows)], 2 + pairs + i)
        for i in range(2)
    ]

    def merge(part):
        for cols in (slice(0, 512), slice(512, width)) if part == 0 else ():
            weight = wo[:, :, cols].reshape(width, cols.stop - cols.start)
            resid[:, cols] = hidden[:, cols].astype(jnp.float32) + dot_nn(att_own[...], weight)

        def second_rows(i, carry):
            rows = aligned(i, 64)
            second[piece, rows, :] = layer_norm(resid[rows, :], second_gain, second_shift).astype(bf16)
            return carry

        lax.fori_loop(part * part_rows // 64, (part + 1) * part_rows // 64, second_rows, 0)
        if part == 1:
            local(resid, resid_out, 12).start()

    def flip_normed():
        def body(i, carry):
            normed_t[aligned(i, 128), :] = normed[:, aligned(i, 128)].T
            return carry

        lax.fori_loop(0, width // 128, body, 0)
        local(normed_t, normed_t_out, 8).start()
        local(lse, lse_out, 10).start()

    def flip_second(half):
        def body(i, carry):
            second_t[aligned(i, 128), half_rows(half)] = second[half, :, aligned(i, 128)].T
            return carry

        lax.fori_loop(0, width // 128, body, 0)

    def flip_att():
        def body(i, carry):
            att_t[aligned(i, 128), :] = att_own[:, aligned(i, 128)].T
            return carry

        lax.fori_loop(0, width // 128, body, 0)
        local(att_t, att_t_out, 11).start()
        flip_second(piece)

    def u_here():
        local(u_own, u_all.at[me], 2).wait()
        all_here_load((3,), u_all, wu, 36)

    unit = 512
    fifth = act.shape[1] // unit // 5

    def expand(half, begin):
        at = half_rows(half)

        def body(i, carry):
            cols = aligned(i, unit)
            weight = wu[:, :, cols].reshape(width, unit)
            up = dot_nn(second[half], weight) + bias[:, cols]
            cdf = 0.5 * (1.0 + lax.erf(up * (0.5 ** 0.5)))
            pdf = jnp.exp(up * up * -0.5) * ((2.0 * math.pi) ** -0.5)
            value = (up * cdf).astype(bf16)
            act[at, cols] = value
            act_t[cols, at] = value.T
            slope[at, cols] = (cdf + up * pdf).astype(bf16)
            return carry

        lax.fori_loop(begin * fifth, (begin + 1) * fifth, body, 0)
        if begin == 4:
            for copy in halves_out(half):
                copy.start()

    def halves_out(half):
        base = 54 if half is piece else 56
        at = half_rows(half)
        return (
            local(act.at[at], act_out.at[at], base),
            local(slope.at[at], slope_out.at[at], base + 1),
        )

    def second_here():
        for copy in second_x:
            copy.wait_recv()

    def flip_last():
        flip_second(other)
        local(second_t, second_t_out, 13).start()

    def dy_here():
        cot_x.wait_recv()
        local(dy.at[other], dy_all, 4).start()

    def grad_down(i):
        h, at = i // 2, slice(i % 2 * UNIT, (i % 2 + 1) * UNIT)

        def left(j):
            begin = lambda block: pl.multiple_of((8 * j + block) * 2 * rows + h * rows, 16)
            return jnp.concatenate([act_t[pl.ds(begin(block), rows), :] for block in range(8)], axis=0)

        grad_chunk(parts.at[i % SLOTS], left, lambda: dy[:, :, at].reshape(length, UNIT))

    sums_x = [
        pltpu.make_async_remote_copy(
            src_ref=parts.at[i % SLOTS, 1 - core], dst_ref=core_in.at[i], send_sem=x_send.at[4 + pairs + i],
            recv_sem=x_recv.at[4 + pairs + i], device_id=peers[4], device_id_type=MESH,
        )
        for i in range(4)
    ]

    def sum_down(i):
        core_in[i] += parts[i % SLOTS, core]
        sums_x[i].wait_send()
        local(core_in.at[i], down_sums.at[i], 50 + i).start()

    def outputs():
        for i in range(4):
            local(core_in.at[i], down_sums.at[i], 50 + i).wait()
        local(dy.at[other], dy_all, 4).wait()
        local(d_own, d_all.at[me], 3).wait()
        local(normed_t, normed_t_out, 8).wait()
        local(packed, packed_out, 9).wait()
        local(lse, lse_out, 10).wait()
        for copy in att_outs:
            copy.wait()
        local(att_t, att_t_out, 11).wait()
        local(resid, resid_out, 12).wait()
        local(second_t, second_t_out, 13).wait()
        for half in (piece, other):
            for copy in halves_out(half):
                copy.wait()

    act_now = functools.partial
    steps = [hidden_x.start, cot_x.start]
    steps += [act_now(pick_units, g) for g in range(4)]
    steps += [act_now(norm_rows, hidden, piece, part) for part in range(2)]
    steps += [act_now(write_marks, starts, key_marks, query_marks), lambda: None]
    steps += [hidden_x.wait_recv]
    steps += [act_now(norm_rows, hid_other, other, part) for part in range(2)]
    steps += [q_here, act_now(loaded, q_all, wq, 20), act_now(project, 0, 1), act_now(project, 1, 3)]
    for p in range(pairs):
        steps += [act_now(attend_other, p), att_x[p].start]
    steps += [act_now(attend_own, p) for p in range(pairs - 1)]
    steps += [o_here, act_now(attend_own, pairs - 1), att_here]
    steps += [act_now(merge, 0), second_x[0].start, act_now(merge, 1), second_x[1].start]
    steps += [flip_normed, flip_att, u_here, act_now(loaded, u_all, wu, 36)]
    steps += [act_now(expand, piece, i) for i in range(5)]
    steps += [second_here, flip_last]
    steps += [act_now(expand, other, i) for i in range(5)]
    steps += [dy_here]
    for i in range(4):
        steps += [act_now(grad_down, i), sums_x[i].start]
        if i:
            steps += [sums_x[i - 1].wait_recv, act_now(sum_down, i - 1)]
    steps += [sums_x[3].wait_recv, act_now(sum_down, 3), outputs, act_now(all_here, (4, 5))]
    moves = (
        lambda w: pass_on(w, 0),
        lambda w: to_y(w, z, True).start(),
        lambda w: to_core(w, z, 0, True).start(),
        relay_z,
        relay_y,
    )
    for i, step in enumerate(steps):
        for kind, *where in FORWARD_MOVES[i]:
            moves[kind](*where)
        step()
        if i == 1:
            first_copies()
    for w in range(len(own)):
        all_gone(w)
    for copy in [hidden_x, cot_x] + second_x + att_x:
        copy.wait_send()


def forward(hidden, cot, starts, gain1, shift1, gain2, shift2, bias, qkv, out, up, down):
    own_rows, width = hidden.shape
    length = 2 * own_rows
    cols = qkv.shape[1] // 2
    units = up.shape[1] // 2
    rows = up.shape[0]
    bf16, f32 = jnp.bfloat16, jnp.float32
    shards = lax.axis_size("rows")
    head_rows = 16
    outs = [
        ((shards, rows, cols), bf16),
        ((shards, rows, width), bf16),
        ((shards, rows, units), bf16),
        ((shards, down.shape[0] // 2, width), bf16),
        ((own_rows, width), bf16),
        ((4, 2, ROWS_Z, rows, UNIT), bf16),
        ((width, length), bf16),
        ((length, cols), bf16),
        ((head_rows, length), f32),
        ((length, cols // 3), bf16),
        ((width, own_rows), bf16),
        ((own_rows, width), f32),
        ((width, length), bf16),
        ((length, units), bf16),
        ((length, units), bf16),
    ]
    scratch = [
        ((own_rows, width), bf16),
        ((length, width), bf16),
        ((shards, rows, cols), bf16),
        ((shards, rows, width), bf16),
        ((shards, rows, units), bf16),
        ((length, cols), bf16),
        ((length, PAIR), bf16),
        ((length, PAIR), bf16),
        ((own_rows, cols // 3), bf16),
        ((own_rows, width), bf16),
        ((own_rows, width), f32),
        ((2, own_rows, width), bf16),
        ((length, units), bf16),
        ((units, length), bf16),
        ((length, units), bf16),
        ((width, length), bf16),
        ((width, own_rows), bf16),
        ((width, length), bf16),
        ((head_rows, length), f32),
        ((rows, 2 * units), bf16),
        ((rows, cols), bf16),
        ((rows, width), bf16),
        ((rows, units), bf16),
        ((2 * rows, width), bf16),
        ((2, own_rows, width), bf16),
        ((1, units), f32),
        ((SLOTS, 2, 2, ROWS_Z, rows, UNIT), bf16),
        ((4, 2, ROWS_Z, rows, UNIT), bf16),
    ]
    vmem = pl.BlockSpec(memory_space=pltpu.VMEM)
    anywhere = pl.BlockSpec(memory_space=pl.ANY)
    smem = pl.BlockSpec(memory_space=pltpu.SMEM)
    dma = pltpu.SemaphoreType.DMA
    x_copies = 8 + cols // (3 * PAIR)
    return pl.pallas_call(
        forward_kernel,
        out_shape=[jax.ShapeDtypeStruct(shape, kind) for shape, kind in outs],
        in_specs=[vmem, anywhere, smem] + [vmem] * 5 + [anywhere] * 4,
        out_specs=[anywhere] * len(outs),
        scratch_shapes=[pltpu.VMEM(shape, kind) for shape, kind in scratch]
        + [dma((58,)), dma((108,)), dma((108,)), dma((x_copies,)), dma((x_copies,))],
        compiler_params=pltpu.CompilerParams(
            collective_id=1, has_side_effects=True, vmem_limit_bytes=60 * 1024 * 1024
        ),
        name="forward",
    )(hidden, cot, starts, gain1, shift1, gain2, shift2, bias, qkv, out, up, down)


BACKWARD_MOVES = (
    ((1, 0), (2, 0), (3, 0), (0, 0),),
    (),
    (),
    (),
    (),
    (),
    (),
    ((2, 1), (1, 1),),
    (),
    (),
    (),
    (),
    (),
    ((4, 0), (3, 1), (0, 1),),
    ((5, 0),),
    ((2, 2),),
    (),
    ((6, 0), (1, 2),),
    ((7, 0), (4, 1), (3, 2),),
    (),
    (),
    ((0, 2),),
    (),
    (),
    (),
    (),
    (),
    (),
    (),
    (),
    ((2, 3), (5, 1),),
    (),
    (),
    ((8, 0), (4, 2), (9, 0), (3, 3),),
    (),
    (),
    ((5, 2), (10, 0), (6, 1), (1, 3),),
    (),
    (),
    (),
    ((11, 0),),
    (),
    (),
    ((7, 1), (0, 3), (8, 1), (4, 3), (12, 0), (5, 3),),
    (),
    (),
    ((6, 2),),
    (),
    (),
    (),
    ((9, 1),),
    (),
    (),
    (),
    ((7, 2), (13, 0), (14, 0), (10, 1), (8, 2), (11, 1), (6, 3), (9, 2), (12, 1), (7, 3), (10, 2), (13, 1), (11, 2), (9, 3), (14, 1),),
    ((8, 3), (12, 2), (10, 3),),
    (),
    (),
    ((13, 2),),
    ((11, 3), (14, 2), (12, 3), (13, 3),),
    ((14, 3),),
)


def thirds(value):
    high = value.astype(jnp.bfloat16)
    rest = value - high.astype(jnp.float32)
    middle = rest.astype(jnp.bfloat16)
    return high, middle, (rest - middle.astype(jnp.float32)).astype(jnp.bfloat16)


def norm_back(values, gain, grad):
    centred = values - jnp.mean(values, axis=-1, keepdims=True)
    scale = lax.rsqrt(jnp.mean(centred * centred, axis=-1, keepdims=True) + 1e-05)
    unit = centred * scale
    scaled = grad * gain
    mean_one = jnp.mean(scaled, axis=-1, keepdims=True)
    mean_two = jnp.mean(scaled * unit, axis=-1, keepdims=True)
    d_values = scale * (scaled - mean_one - unit * mean_two)
    d_gain = jnp.sum(grad * unit, axis=0, keepdims=True)
    d_shift = jnp.sum(grad, axis=0, keepdims=True)
    return d_values, d_gain, d_shift


def backward_kernel(
    starts, gain1, gain2, hidden, cot, dy_other, q_all, o_all, u_all, d_all, down_sums, normed_t, packed, lse_in, att_in, att_t_in,
    resid, second_t, act, slope,
    output, grad_hidden, units_out, pairs_out, small_out,
    lhs, att_t, att_own, half_act, wide, wd, wu, dy, first, second, d_att, x_in0, x_in1, x_out0, down_own,
    parts, core_in, core_in_q, y_in, y_in_q, z_in, z_in_q, down_early, lse_rows, lse, key_marks, query_marks, acc_k, acc_v, bias_sum, early, late,
    early_near, late_near, early_all, late_all, small,
    local_sem, a_send, a_recv, b_send, b_recv, c_send, c_recv, g_send, g_recv, x_send, x_recv,
    s_send, s_recv, keep_sem,
):
    bf16, f32 = jnp.bfloat16, jnp.float32
    z, y, core = place_of()
    piece = lax.axis_index("blk")
    other = 1 - piece
    own_rows, width = first.shape
    length = 2 * own_rows
    branch = half_act.at[:, pl.ds(0, width)]
    units = wide.shape[1]
    d_width = d_att.shape[1]
    cols = 3 * d_width
    pairs = d_width // PAIR
    near = z + 1 - 2 * lax.rem(z, 2)
    far = lax.rem(z + 2, ROWS_Z)
    peer_core, peer_y = {"rows": row_of(z, y, 1 - core)}, {"rows": row_of(z, 1 - y, core)}
    peer_near, peer_far = {"rows": row_of(near, y, core)}, {"rows": row_of(far, y, core)}
    peer_x = {"blk": other}
    group = [peer_core, peer_y, {"rows": row_of(z, 1 - y, 1 - core)}]
    line = [
        {"rows": row_of(z + k, y, core), "blk": lax.rem(piece + n, 2)} for n in range(2) for k in range(ROWS_Z) if n or k
    ]
    wide_chunks = core_in.shape[0]
    chunks = wide_chunks + pairs
    first_gain, second_gain = gain1[...].reshape(1, width), gain2[...].reshape(1, width)
    half_rows = lambda half: pl.ds(pl.multiple_of(half * own_rows, 128), own_rows)
    part_rows = own_rows // 2

    def remote(src, dst, sends, recvs, index, peer):
        return pltpu.make_async_remote_copy(
            src_ref=src, dst_ref=dst, send_sem=sends.at[index], recv_sem=recvs.at[index],
            device_id=peer, device_id_type=MESH,
        )

    loads = {
        "sums": (down_sums, core_in.at[pl.ds(0, 4)], 0),
        "dy": (cot, dy.at[piece], 1),
        "dy_other": (dy_other, dy.at[other], 2),
        "up": (u_all, wu, 4),
        "act_other": (act.at[half_rows(other)], half_act, 5),
        "act_own": (act.at[half_rows(piece)], half_act, 6),
        "resid": (resid, second, 7),
        "lse": (lse_in, lse_rows.at[pl.ds(0, 16)], 8),
        "second_t": (second_t, lhs, 9),
        "att_t": (att_t_in, att_t, 10),
        "out": (o_all, wd.at[pl.ds(0, width)], 11),
        "normed_t": (normed_t, wd.at[pl.ds(width, width), pl.ds(0, length)], 12),
        "qkv": (q_all, wu.at[:, pl.ds(0, cols)], 13),
        "packed": (packed, wide.at[:, pl.ds(0, cols)], 14),
        "hidden": (hidden, branch, 15),
        "output": (second, output, 16),
        "grad_hidden": (first, grad_hidden, 17),
        "att": (att_in, att_own, 18),
    }

    def local(name):
        src, dst, index = loads[name]
        return pltpu.make_async_copy(src, dst, local_sem.at[index])

    z_first = (0, 1, 8)
    mine, theirs = pl.ds(2 * lax.rem(z, 2), 2), pl.ds(2 - 2 * lax.rem(z, 2), 2)
    place, far_place = z_place(z), z_place(far)
    order = tuple(range(chunks))

    def buffers(i):
        if i < wide_chunks:
            return core_in.at[i], y_in.at[i], z_in.at[i], units_out.at[:, i], UNIT
        i -= wide_chunks
        return core_in_q.at[i], y_in_q.at[i], z_in_q.at[i], pairs_out.at[:, i], 3 * PAIR

    def copy_a(i):
        into, _, _, _, n = buffers(i)
        return remote(parts.at[i % SLOTS, 1 - core, :, :, :, pl.ds(0, n)], into, a_send, a_recv, i, peer_core)

    def copy_b(i):
        sums, by_y, by_z, _, _ = buffers(i)
        if i < 4 and i not in z_first:
            sums = down_sums.at[i]
        if i in z_first:
            return remote(sums.at[1 - y, place], by_z.at[2], b_send, b_recv, i, peer_y)
        return remote(sums.at[1 - y], by_y, b_send, b_recv, i, peer_y)

    def copies_c(i, step):
        sums, by_y, by_z, _, _ = buffers(i)
        index = 4 * i + 2 * step
        if i not in z_first:
            if step == 0:
                return [remote(by_y.at[theirs], by_z.at[pl.ds(0, 2)], c_send, c_recv, index, peer_near)]
            return [remote(by_y.at[far_place], by_z.at[2], c_send, c_recv, index, peer_far)]
        if step == 0:
            sums = down_sums.at[i] if i < 4 else sums
            return [
                remote(sums.at[v, theirs], by_y.at[pl.ds(2 * v, 2)], c_send, c_recv, index + v, peer_near)
                for v in range(2)
            ]
        return [remote(sums.at[v, far_place], by_z.at[v], c_send, c_recv, index + v, peer_far) for v in range(2)]

    def copy_g(i):
        _, _, by_z, out, _ = buffers(i)
        return remote(by_z.at[0], out.at[piece], g_send, g_recv, i, peer_x)

    def keep_g(i):
        _, _, by_z, out, _ = buffers(i)
        return pltpu.make_async_copy(by_z.at[0], out.at[piece], keep_sem.at[i])

    unread = ["sums"]

    def move(i, stage):
        sums, by_y, by_z, _, n = buffers(i)
        if i < 4 and stage and unread:
            local(unread.pop()).wait()
        if stage == 0:
            slot = i % SLOTS
            if i >= 4:
                copy_a(i).wait_recv()
                sums[1 - y] += parts[slot, core, 1 - y, :, :, :n]
                if i in z_first:
                    sums[y] += parts[slot, core, y, :, :, :n]
            if i in z_first:
                for copy in copies_c(i, 0):
                    copy.start()
            else:
                copy_b(i).start()
            if i >= 4:
                if i not in z_first:
                    sums[y] += parts[slot, core, y, :, :, :n]
                copy_a(i).wait_send()
        elif i in z_first and stage < 3:
            for v, copy in enumerate(copies_c(i, stage - 1)):
                copy.wait_recv()
                if stage == 1:
                    sums[v, mine] += by_y[2 * v : 2 * v + 2]
                else:
                    sums[v, place] += by_z[v]
            for copy in copies_c(i, 1) if stage == 1 else [copy_b(i)]:
                copy.start()
        elif stage == 1:
            copy_b(i).wait_recv()
            by_y[...] += sums[y]
            copies_c(i, 0)[0].start()
        elif stage == 2:
            copies_c(i, 0)[0].wait_recv()
            by_y[mine] += by_z[0:2]
            copies_c(i, 1)[0].start()
        else:
            if i in z_first:
                copy_b(i).wait_recv()
                total = sums[y, place].astype(f32) + by_z[2].astype(f32)
            else:
                copies_c(i, 1)[0].wait_recv()
                total = by_y[place].astype(f32) + by_z[2].astype(f32)
            by_z[0] = total.astype(bf16)
            copy_g(i).start()
            keep_g(i).start()

    tile = 512

    def tile_loads(i):
        at = aligned(i, tile)
        return (
            pltpu.make_async_copy(d_all.at[at], wd.at[at], local_sem.at[19 + 2 * i]),
            pltpu.make_async_copy(slope.at[:, at], wide.at[:, at], local_sem.at[20 + 2 * i]),
        )

    local("act_other").start()
    for i in range(units // tile):
        tile_loads(i)[0].start()
    local("dy").start()
    local("dy_other").start()
    for i in range(units // tile):
        tile_loads(i)[1].start()
    greet(group + line)

    def ready_units():
        local("act_other").wait()
        for i in range(units // tile):
            tile_loads(i)[0].wait()
        for name in ("sums", "up", "second_t", "resid", "lse", "att_t"):
            local(name).start()

    halves = (slice(0, 512), slice(512, width))

    def d_units(begin, end):
        if begin == 0:
            local("dy").wait()
            local("dy_other").wait()

        def body(i, carry):
            tile_loads(i)[1].wait()
            at = aligned(i, tile)
            value = dot_nt(dy[...].reshape(length, width), wd[at, :]) * wide[:, at].astype(f32)
            low = value.astype(bf16)
            wide[:, at] = low
            bias_sum[:, at] = jnp.sum(low.astype(f32), axis=0, keepdims=True)
            return carry

        lax.fori_loop(begin, end, body, 0)

    def d_second(half, part, target):
        if part == 0 and target is x_out0:
            local("up").wait()
        at = halves[part]
        target[:, at] = dot_nt(wide[half_rows(half), :], wu[at, :]).astype(target.dtype)

    def exchange(part, index):
        at = pl.ds(halves[part].start, halves[part].stop - halves[part].start)
        return remote(x_out0.at[:, at], x_in0.at[:, at], x_send, x_recv, index, peer_x)

    second_x = [exchange(part, part) for part in range(2)]
    normed_x = [exchange(part, 2 + part) for part in range(2)]
    first_cols, rest_cols = (pl.ds(at.start, at.stop - at.start) for at in halves)
    down_x = [
        remote(down_early, x_in1.at[:, first_cols], x_send, x_recv, 4, peer_x),
        remote(dy.at[other, :, rest_cols], x_in1.at[:, rest_cols], x_send, x_recv, 5 + pairs, peer_x),
    ]
    att_x = [
        remote(
            x_out0.at[:, pl.ds(p * PAIR, PAIR)], d_att.at[half_rows(piece), pl.ds(p * PAIR, PAIR)],
            x_send, x_recv, 5 + p, peer_x,
        )
        for p in range(pairs)
    ]

    def d_second_own():
        for part in range(2):
            d_second(piece, part, first)
        local("qkv").start()

    def down_first():
        down_early[...] = dot_nn(half_act[...], wd[:, halves[0]]).astype(bf16)

    def down_other():
        dy[other, :, halves[1]] = dot_nn(half_act[...], wd[:, halves[1]]).astype(bf16)
        local("act_own").start()

    def down_mine():
        local("act_own").wait()
        for at in halves:
            down_own[:, at] = dot_nn(half_act[...], wd[:, at]).astype(bf16)
        local("out").start()
        local("normed_t").start()

    def chunk(i, left, right):
        grad_chunk(parts.at[i % SLOTS], left, right)
        copy_a(i).start()

    def grad_up(i):
        if i == 0:
            local("second_t").wait()
        left = lambda j: lhs[pl.ds(8 * j, 8)].reshape(8 * lhs.shape[1], length)
        chunk(4 + i, left, lambda: wide[:, i * UNIT : (i + 1) * UNIT])
        if i == 3:
            local("packed").start()
            local("att").start()

    step = 64

    def back_two(part):
        if part == 0:
            local("resid").wait()
            for copy in second_x:
                copy.wait_recv()

        def body(i, carry):
            rows = aligned(i, step)
            grad = first[rows, :] + x_in0[rows, :].astype(f32)
            d_values, d_gain, d_shift = norm_back(second[rows, :], second_gain, grad)
            total = dy[piece, rows, :].astype(f32) + d_values
            first[rows, :] = total
            branch[rows, :] = total.astype(bf16)
            early[0:1, :] += d_gain
            early[1:2, :] += d_shift
            return carry

        steps_each = part_rows // step
        if part == 0:
            early[...] = jnp.zeros_like(early)
        lax.fori_loop(part * steps_each, (part + 1) * steps_each, body, 0)

    def d_attended(half):
        rows = pl.ds(pl.multiple_of(half * d_width, 128), d_width)
        return dot_nt(branch[...], wd[rows, :]).astype(bf16)

    def d_att_other():
        local("out").wait()
        for copy in second_x:
            copy.wait_send()
        x_out0[:, :d_width] = d_attended(other)

    def d_att_own():
        d_att[half_rows(piece), :] = d_attended(piece)

    def grad_out(i):
        if i == 0:
            local("att_t").wait()
        left = lambda j: att_t[pl.ds(8 * j, 8)].reshape(8 * att_t.shape[1], own_rows)
        chunk(8 + i, left, lambda: branch[:, i * UNIT : (i + 1) * UNIT])
        if i == 1:
            local("hidden").start()

    first_lanes = head_lanes(PAIR)
    query_chunk = 256

    def pair_cols(p):
        return tuple(slice(t * d_width + PAIR * p, t * d_width + PAIR * (p + 1)) for t in range(3))

    def att_here(p):
        if p == 0:
            for name in ("lse", "packed", "normed_t", "att"):
                local(name).wait()
            lse[...] = lse_rows[...].T
        att_x[p].wait_recv()
        acc_k[...] = jnp.zeros_like(acc_k)
        acc_v[...] = jnp.zeros_like(acc_v)

    lane = lax.broadcasted_iota(jnp.int32, (1, PAIR), 1)
    lane = jnp.where(lane < HEAD_DIM, lane, lane - HEAD_DIM)

    def marked(value, marks):
        for at, part in enumerate(thirds(value)):
            marks = jnp.where(lane == at, part, marks)
        return marks

    def attend_back(p):
        at_q, at_k, at_v = pair_cols(p)
        heads = slice(p * PAIR, (p + 1) * PAIR)
        keys_t = wide[:, at_k].T

        def one_chunk(i, carry):
            rows = aligned(i, query_chunk)
            keys, values, queries = wide[:, at_k], wide[:, at_v], wide[rows, at_q]
            grads = d_att[rows, heads]
            attended = att_own[rows, heads]
            products = grads.astype(f32) * attended.astype(f32)
            nothing = jnp.zeros_like(queries)
            parts_q = []
            for h in range(2):
                here = first_lanes[h]
                dots = jnp.sum(jnp.where(here, products, 0.0), axis=1, keepdims=True)
                top = lse[rows, 2 * p + h : 2 * p + h + 1]
                one_q = jnp.where(here, queries, marked(-top, query_marks[rows, :]))
                one_g = jnp.where(here, grads, marked(-dots, nothing))
                probs = jnp.exp(dot_nt(jnp.where(here, keys, key_marks[...]), one_q))
                d_scores = (probs * dot_nt(jnp.where(here, values, key_marks[...]), one_g)).astype(bf16)
                acc_v[...] += dot_nn(probs.astype(bf16), jnp.where(here, grads, nothing))
                acc_k[...] += dot_nn(d_scores, jnp.where(here, queries, nothing))
                parts_q.append(dot_nn(keys_t[h * HEAD_DIM : (h + 1) * HEAD_DIM], d_scores))
            d_queries = jnp.concatenate(parts_q, axis=0).T * HEAD_DIM ** (-0.5)
            wide[rows, at_q] = d_queries.astype(bf16)
            return carry

        lax.fori_loop(0, length // query_chunk, one_chunk, 0)
        wide[:, at_k] = acc_k[...].astype(bf16)
        wide[:, at_v] = acc_v[...].astype(bf16)

    def grad_pair(p):
        n = 8 * parts.shape[4]
        left = lambda j: wd[pl.ds(pl.multiple_of(width + j * n, 64), n), :length]
        chunk(10 + p, left, lambda: jnp.concatenate([wide[:, at] for at in pair_cols(p)], axis=1))

    def down_here():
        for copy in down_x:
            copy.wait_recv()

    def write_output():
        def body(i, carry):
            rows = aligned(i, step)
            second[rows, :] += down_own[rows, :].astype(f32) + x_in1[rows, :].astype(f32)
            return carry

        lax.fori_loop(0, own_rows // step, body, 0)
        local("output").start()

    def d_normed(half, part, target):
        if part == 0 and target is x_out0:
            local("qkv").wait()
            for copy in att_x:
                copy.wait_send()
        at = halves[part]
        target[:, at] = dot_nt(wide[half_rows(half), :cols], wu[at, :cols]).astype(target.dtype)

    def d_normed_own():
        local("output").wait()
        for part in range(2):
            d_normed(piece, part, second)

    def back_one(part):
        if part == 0:
            local("hidden").wait()
            late[...] = jnp.zeros_like(late)
            for copy in normed_x:
                copy.wait_recv()

        def body(i, carry):
            rows = aligned(i, step)
            grad = second[rows, :] + x_in0[rows, :].astype(f32)
            d_values, d_gain, d_shift = norm_back(branch[rows, :].astype(f32), first_gain, grad)
            first[rows, :] += d_values
            late[0:1, :] += d_gain
            late[1:2, :] += d_shift
            return carry

        steps_each = part_rows // step
        lax.fori_loop(part * steps_each, (part + 1) * steps_each, body, 0)
        if part == 1:
            local("grad_hidden").start()

    def small_near(value, near_slots, base):
        own_slot = 2 * y + core
        return [
            remote(value, near_slots.at[own_slot], s_send, s_recv, base + k, peer) for k, peer in enumerate(group)
        ]

    def small_line(all_slots, base):
        own_slot = z * 2 + piece
        return [
            remote(all_slots.at[own_slot], all_slots.at[own_slot], s_send, s_recv, base + 3 + k, peer)
            for k, peer in enumerate(line)
        ]

    def small_one(value, near_slots, base):
        near_slots[2 * y + core] = value[...]
        for copy in small_near(value, near_slots, base):
            copy.start()

    def small_two(value, near_slots, all_slots, base):
        for copy in small_near(value, near_slots, base):
            copy.wait()
        all_slots[z * 2 + piece] = ((near_slots[0] + near_slots[1]) + near_slots[2]) + near_slots[3]
        for copy in small_line(all_slots, base):
            copy.start()

    def small_three(all_slots, base, at):
        for copy in small_line(all_slots, base):
            copy.wait()
        n = all_slots.shape[1]
        for x in range(2):
            total = ((all_slots[x] + all_slots[2 + x]) + all_slots[4 + x]) + all_slots[6 + x]
            small[x, at : at + n, :] = total

    def early_one():
        early[2:3, :] = bias_sum[:, :width]
        early[3:4, :] = bias_sum[:, width:]
        small_one(early, early_near, 0)

    call = functools.partial
    steps = [ready_units, down_first, down_x[0].start, call(d_units, 0, 2), call(d_units, 2, 4), call(d_units, 4, 5)]
    for part in range(2):
        steps += [call(d_second, other, part, x_out0), second_x[part].start]
    steps += [call(grad_up, 0), call(grad_up, 1), d_second_own, down_other, call(grad_up, 2), call(grad_up, 3), down_mine]
    steps += [call(write_marks, starts, key_marks, query_marks), call(back_two, 0), call(back_two, 1), d_att_other]
    steps += [copy.start for copy in att_x]
    steps += [d_att_own, down_x[1].start, early_one, call(grad_out, 0), call(grad_out, 1)]
    for p in range(pairs):
        steps += [call(att_here, p)] + [call(attend_back, p)]
        if p < 3:
            steps += [call(grad_pair, p)]
        if p == 1:
            steps += [call(small_two, early, early_near, early_all, 0)]
    for part in range(2):
        steps += [call(d_normed, other, part, x_out0), normed_x[part].start]
    steps += [call(grad_pair, 3), call(grad_pair, 4), down_here, write_output, d_normed_own]
    steps += [call(back_one, 0), call(back_one, 1), call(small_one, late, late_near, 10)]
    steps += [call(small_three, early_all, 0, 2), call(small_two, late, late_near, late_all, 10)]
    steps += [call(small_three, late_all, 10, 0)]
    for i, one in enumerate(steps):
        for where in BACKWARD_MOVES[i]:
            move(*where)
        one()
    small_keep = pltpu.make_async_copy(small, small_out, keep_sem.at[chunks])
    small_keep.start()
    for where in BACKWARD_MOVES[len(steps)]:
        move(*where)
    for i in range(chunks):
        copy_b(i).wait_send()
        for copy in copies_c(i, 0) + copies_c(i, 1):
            copy.wait_send()
        copy_g(i).wait()
        keep_g(i).wait()
    small_keep.wait()
    for copy in down_x + normed_x:
        copy.wait_send()
    local("grad_hidden").wait()


def backward(starts, gain1, gain2, hidden, cot, dy_other, q_all, o_all, u_all, d_all, *kept):
    bf16, f32 = jnp.bfloat16, jnp.float32
    own_rows, width = hidden.shape
    length = 2 * own_rows
    cols, units = q_all.shape[1], u_all.shape[1]
    rows = width // 16
    wide_units, pairs = 10, cols // (3 * PAIR)
    pair_cols = 3 * PAIR
    outs = [
        ((own_rows, width), f32),
        ((own_rows, width), f32),
        ((2, wide_units, rows, UNIT), bf16),
        ((2, pairs, rows, pair_cols), bf16),
        ((2, 6, width), f32),
    ]
    token = ((own_rows, width), bf16)
    scratch = [
        ((16, rows, length), bf16),
        ((16, rows, own_rows), bf16),
        ((length, cols // 3), bf16),
        ((own_rows, units), bf16),
        ((length, units), bf16),
        ((units, width), bf16),
        ((width, units), bf16),
        ((2, own_rows, width), bf16),
        ((own_rows, width), f32),
        ((own_rows, width), f32),
        ((length, cols // 3), bf16),
        token, token, token, token,
        ((SLOTS, 2, 2, ROWS_Z, rows, UNIT), bf16),
        ((wide_units, 2, ROWS_Z, rows, UNIT), bf16),
        ((pairs, 2, ROWS_Z, rows, pair_cols), bf16),
        ((wide_units, ROWS_Z, rows, UNIT), bf16),
        ((pairs, ROWS_Z, rows, pair_cols), bf16),
        ((wide_units, 3, rows, UNIT), bf16),
        ((pairs, 3, rows, pair_cols), bf16),
        ((own_rows, 512), bf16),
        ((PAIR, length), f32),
        ((length, PAIR), f32),
        ((length, PAIR), bf16),
        ((length, PAIR), bf16),
        ((length, PAIR), f32),
        ((length, PAIR), f32),
        ((1, units), f32),
        ((4, width), f32),
        ((2, width), f32),
        ((4, 4, width), f32),
        ((4, 2, width), f32),
        ((8, 4, width), f32),
        ((8, 2, width), f32),
        ((2, 6, width), f32),
    ]
    vmem = pl.BlockSpec(memory_space=pltpu.VMEM)
    anywhere = pl.BlockSpec(memory_space=pl.ANY)
    smem = pl.BlockSpec(memory_space=pltpu.SMEM)
    chunks = wide_units + pairs
    dma = lambda n: pltpu.SemaphoreType.DMA((n,))
    sems = [29] + [chunks] * 4 + [4 * chunks] * 2 + [chunks] * 2 + [6 + pairs] * 2 + [20, 20, chunks + 1]
    return pl.pallas_call(
        backward_kernel,
        out_shape=[jax.ShapeDtypeStruct(shape, kind) for shape, kind in outs],
        in_specs=[smem, vmem, vmem] + [anywhere] * (7 + len(kept)),
        out_specs=[anywhere] * len(outs),
        scratch_shapes=[pltpu.VMEM(shape, kind) for shape, kind in scratch] + [dma(n) for n in sems],
        compiler_params=pltpu.CompilerParams(
            collective_id=2, has_side_effects=True, vmem_limit_bytes=60 * 1024 * 1024
        ),
        name="backward",
    )(starts, gain1, gain2, hidden, cot, dy_other, q_all, o_all, u_all, d_all, *kept)


def finish_kernel(
    raw_output, raw_grad, units_lo, units_hi, pairs_in, small,
    output, grad_hidden, qkv, out, up, down, gain1, shift1, gain2, shift2, bias,
):
    f32 = jnp.float32
    step = pl.program_id(0)
    output[0] = raw_output[...]
    grad_hidden[0] = raw_grad[...]
    rows = out.shape[0]
    width = small.shape[2]
    units_in = (units_lo, units_hi)

    def mixed(first, second):
        each = first.shape[1] // 4
        blocks = []
        for j in range(4):
            at = slice(j * each, (j + 1) * each)
            blocks += [first[:, at].astype(f32), second[:, at].astype(f32)]
        return jnp.concatenate(blocks, axis=1)

    for now in range(2):

        @pl.when(step == now)
        def _():
            for i in range(4):
                h, column = divmod(i, 2)
                at = slice(column * UNIT, (column + 1) * UNIT)
                down[h * rows : (h + 1) * rows, at] = units_in[now][0, i].astype(f32)
            for i in range(2):
                chunk = 4 + 2 * now + i
                at = slice(i * 2 * UNIT, (i + 1) * 2 * UNIT)
                up[:, at] = mixed(units_lo[0, chunk], units_hi[0, chunk])
            out[...] = units_lo[0, 8 + now].astype(f32) + units_hi[0, 8 + now].astype(f32)
            pairs = pairs_in.shape[1]
            for block in range(3 * now, 3 * now + 3):
                part, piece = divmod(block, 2)
                for p in range(pairs):
                    at = (block - 3 * now) * pairs * PAIR + p * PAIR
                    chunk = pairs_in[piece, p, :, part * PAIR : (part + 1) * PAIR]
                    qkv[:, at : at + PAIR] = chunk.astype(f32)

    @pl.when(step == 0)
    def _():
        for i, ref in enumerate((gain1, shift1, gain2, shift2)):
            ref[...] = (small[0, i : i + 1, :] + small[1, i : i + 1, :]).reshape(width)
        for g in range(2):
            for j in range(2):
                at = slice(j * UNIT, (j + 1) * UNIT)
                lo, hi = small[0, 4 + g : 5 + g, at], small[1, 4 + g : 5 + g, at]
                begin = (2 * g + j) * 2 * UNIT
                bias[begin : begin + 2 * UNIT] = mixed(lo, hi).reshape(2 * UNIT)


def finish(raw_output, raw_grad, units_in, pairs_in, small):
    f32 = jnp.float32
    own_rows, width = raw_output.shape
    rows = units_in.shape[2]
    shapes = [
        (1, own_rows, width), (1, own_rows, width), (rows, 3 * width), (rows, width), (rows, 8 * UNIT),
        (4 * rows, width), (width,), (width,), (width,), (width,), (8 * UNIT,),
    ]
    token = pl.BlockSpec((own_rows // 2, width), lambda s: (s, 0))
    token_out = pl.BlockSpec((1, own_rows // 2, width), lambda s: (0, s, 0))
    columns = lambda n: pl.BlockSpec((rows, n // 2), lambda s: (0, s))
    fixed = lambda shape: pl.BlockSpec(shape, lambda s: (0,) * len(shape))
    half = lambda i: pl.BlockSpec((1,) + units_in.shape[1:], lambda s: (i, 0, 0, 0))
    return pl.pallas_call(
        finish_kernel,
        grid=(2,),
        out_shape=[jax.ShapeDtypeStruct(shape, f32) for shape in shapes],
        in_specs=[token, token, half(0), half(1), fixed(pairs_in.shape), fixed(small.shape)],
        out_specs=[
            token_out, token_out, columns(3 * width), columns(width), columns(8 * UNIT),
            pl.BlockSpec((2 * rows, width), lambda s: (s, 0)),
        ] + [fixed(shape) for shape in shapes[6:]],
        compiler_params=pltpu.CompilerParams(vmem_limit_bytes=60 * 1024 * 1024),
        name="finish",
    )(raw_output, raw_grad, units_in, units_in, pairs_in, small)


def split_layer(
    hidden, starts, first_gain, first_shift, qkv_weight, out_weight, second_gain, second_shift,
    up_weight, hidden_bias, down_weight, cotangent,
):
    shards = lax.axis_size("rows")
    (
        qkv_all, out_all, up_all, down_all, dy_other, down_sums, normed_t, packed, lse, att, att_t, residual, second_t,
        activated, slope,
    ) = forward(
        hidden[0], cotangent[0], starts, first_gain, first_shift, second_gain, second_shift, hidden_bias,
        qkv_weight, out_weight, up_weight, down_weight,
    )
    whole = lambda w: w.reshape(-1, w.shape[-1])
    blocks = lambda w: w.reshape(shards, -1, w.shape[-1])
    shares = backward(
        starts, first_gain, second_gain, hidden[0], cotangent[0], dy_other, whole(qkv_all), whole(out_all),
        whole(up_all), whole(down_all), down_sums, normed_t, packed, lse, att, blocks(att_t), residual,
        blocks(second_t), activated, slope,
    )
    return tuple(finish(*shares))


def splits_evenly(mesh):
    pieces = mesh.shape["blk"]
    return pieces == 2 and mesh.shape["rows"] == 2 * ROWS_Z * ROWS_Y and HEADS % (2 * pieces) == 0


def solution(mesh):
    in_specs = (
        P("rows", "blk", None),
        P("rows", None),
        P(),
        P(),
        P("rows", None),
        P("rows", None),
        P(),
        P(),
        P("rows", None),
        P(),
        P("rows", None),
        P("rows", "blk", None),
    )
    out_specs = (
        P("rows", "blk", None),
        P("rows", "blk", None),
        P("rows", None),
        P("rows", None),
        P("rows", None),
        P("rows", None),
        P(),
        P(),
        P(),
        P(),
        P(),
    )
    layer = split_layer if splits_evenly(mesh) else on_device
    return jax.shard_map(
        layer, mesh=mesh, in_specs=in_specs, out_specs=out_specs, check_vma=False
    )
```

profile of v0, /device:TPU:0, one launch (start us, length us, event | category | flops | bytes accessed | tf_op | source)
XLA Modules:
  0.0 263.5 jit_solution(17370451205182262194)
XLA Ops:
  0.6 125.6 %forward.1 = (bf16[16,80,1920]{2,1,0:T(8,128)(2,1)}, bf16[16,80,1280]{2,1,0:T(8,128)(2,1)}, bf16[16,80,2560]{2,1,0:T(8,128)(2,1)}, bf16[16,160,1280]{2,1,0:T(8,1...) custom-call(bf16[384,1280]{1,0:T(8,128)(2,1)} %bitcast.11, ...), custom_call_target="tpu_custom_call" | custom-call | tf_op jit(solution)/shard_map/forward/pallas_call | solution.py:900
  126.2 130.3 %backward.1 = (f32[384,1280]{1,0:T(8,128)}, f32[384,1280]{1,0:T(8,128)}, bf16[2,10,80,640]{3,2,1,0:T(8,128)(2,1)}, bf16[2,5,80,384]{3,2,1,0:T(8,128)(2,1)}, f32[2,6,1280]{2,1,0:T(8,128)}) custom-call(s32[1,4]{1,0:T(1,128)} %starts.3, f32[1280]{0:T(1024)} %gain1.3, f32[1280]{0:T(1024)} %gain2.3, bf16[384,1280]{1,0:T(8,128)(2,1)} %bitcast.12, ...), custom_call_target="tpu_custom_call" | custom-call | tf_op jit(solution)/shard_map/backward/pallas_call | solution.py:1550
  256.5 6.5 %finish.1 = (f32[1,384,1280]{2,1,0:T(8,128)}, f32[1,384,1280]{2,1,0:T(8,128)}, f32[80,3840]{1,0:T(8,128)}, f32[80,1280]{1,0:T(8,128)}, f32[80,5120]{1,0:T(8,128)...) custom-call(f32[384,1280]{1,0:T(8,128)} %get-tuple-element.46.raw_ou, ...), custom_call_target="tpu_custom_call" | custom-call | tf_op jit(solution)/shard_map/finish/pallas_call | solution.py:1629
where the time goes:
time: 267 us; the launch traced here: 263 us
  Pallas kernels  262 us (98%)
    pallas_call x1, Pallas kernels, backward(): pl.pallas_call(backward_kernel, out_shape=[jax.ShapeDtypeStruct(shape, ki...  130 us
    pallas_call x1, Pallas kernels, forward(): pl.pallas_call(forward_kernel, out_shape=[jax.ShapeDtypeStruct(shape, kin...  126 us
    pallas_call x1, Pallas kernels, finish(): pl.pallas_call(finish_kernel, grid=(2,), out_shape=[jax.ShapeDtypeStruct(...  6.48 us

commit v1 on v0

--- a/solution.py
+++ b/solution.py
@@ -557,12 +557,12 @@
         copy.wait()
     hidden_x = to_x(hidden, hid_other, 0)
     cot_x = to_x(cot, dy.at[piece], 1)
-    local(o_in, o_own, 1).wait()
-    local(d_mine, d_own, 3).wait()
-    local(u_in, u_wide, 2).wait()
     half_rows = lambda half: pl.ds(pl.multiple_of(half * own_rows, 128), own_rows)
 
     def first_copies():
+        local(o_in, o_own, 1).wait()
+        local(d_mine, d_own, 3).wait()
+        local(u_in, u_wide, 2).wait()
         local(q_own, q_all.at[me], 0).start()
         local(o_own, o_all.at[me], 1).start()
         local(d_own, d_all.at[me], 3).start()

time: 267 us -> 270 us (1.011)
  Pallas kernels: 262 us -> 265 us
    pallas_call x1, Pallas kernels: 126 us -> 129 us  [forward(): pl.pallas_call(forward_kernel, out_shape=[jax.ShapeDtypeStruct(shape, kin...]
where the time goes in v1:
time: 270 us; the launch traced here: 266 us
  Pallas kernels  265 us (98%)
    pallas_call x1, Pallas kernels, backward(): pl.pallas_call(backward_kernel, out_shape=[jax.ShapeDtypeStruct(shape, ki...  130 us
    pallas_call x1, Pallas kernels, forward(): pl.pallas_call(forward_kernel, out_shape=[jax.ShapeDtypeStruct(shape, kin...  129 us
    pallas_call x1, Pallas kernels, finish(): pl.pallas_call(finish_kernel, grid=(2,), out_shape=[jax.ShapeDtypeStruct(...  6.48 us

profile of v1, /device:TPU:0, one launch (start us, length us, event | category | flops | bytes accessed | tf_op | source)
XLA Modules:
  0.0 266.4 jit_solution(12894976803730932704)
XLA Ops:
  0.6 128.9 %forward.1 = (bf16[16,80,1920]{2,1,0:T(8,128)(2,1)}, bf16[16,80,1280]{2,1,0:T(8,128)(2,1)}, bf16[16,80,2560]{2,1,0:T(8,128)(2,1)}, bf16[16,160,1280]{2,1,0:T(8,1...) custom-call(bf16[384,1280]{1,0:T(8,128)(2,1)} %bitcast.11, ...), custom_call_target="tpu_custom_call" | custom-call | tf_op jit(solution)/shard_map/forward/pallas_call | solution.py:900
  129.6 129.8 %backward.1 = (f32[384,1280]{1,0:T(8,128)}, f32[384,1280]{1,0:T(8,128)}, bf16[2,10,80,640]{3,2,1,0:T(8,128)(2,1)}, bf16[2,5,80,384]{3,2,1,0:T(8,128)(2,1)}, f32[2,6,1280]{2,1,0:T(8,128)}) custom-call(s32[1,4]{1,0:T(1,128)} %starts.3, f32[1280]{0:T(1024)} %gain1.3, f32[1280]{0:T(1024)} %gain2.3, bf16[384,1280]{1,0:T(8,128)(2,1)} %bitcast.12, ...), custom_call_target="tpu_custom_call" | custom-call | tf_op jit(solution)/shard_map/backward/pallas_call | solution.py:1550
  259.4 6.5 %finish.1 = (f32[1,384,1280]{2,1,0:T(8,128)}, f32[1,384,1280]{2,1,0:T(8,128)}, f32[80,3840]{1,0:T(8,128)}, f32[80,1280]{1,0:T(8,128)}, f32[80,5120]{1,0:T(8,128)...) custom-call(f32[384,1280]{1,0:T(8,128)} %get-tuple-element.46.raw_ou, ...), custom_call_target="tpu_custom_call" | custom-call | tf_op jit(solution)/shard_map/finish/pallas_call | solution.py:1629
